TPU v7x, 512 devices: a whole 4x8x8 slice. The times are simulated.
512 devices in a mesh: az: 128 (over z, x, y_hi), ch: 4 (over y_lo, core).
Axes of the slice: x: 4, y: 8 (y_hi: 4, y_lo: 2; y = y_hi * 2 + y_lo), z: 8, core: 2. Of those that a mesh axis runs over, the one named last changes fastest.
Arguments:
- features: bfloat16 [256, 512, 256], P(None, 'az'), may hold values from -6 to 6
- conv1_weight: bfloat16 [256, 3, 3, 256], P('ch'), may hold values from -0.125 to 0.125
- conv1_bias: float32 [256], P('ch'), may hold values from -3 to 3
- conv2_weight: bfloat16 [256, 3, 3, 256], P('ch'), may hold values from -0.125 to 0.125
- conv2_bias: float32 [256], P('ch'), may hold values from -3 to 3
- request_cell: int32 [524288], P('az'), may hold values from 0 to 1023, as said below
- corner_slot: int32 [4, 65536], P(None, 'az'), may hold values from 0 to 4095, as said below
- corner_frac: float32 [2, 65536], P(None, 'az'), may hold values from 0 to 1
- expand_weight: bfloat16 [256, 512], P('ch'), may hold values from -0.375 to 0.375
- expand_bias: float32 [512], P('ch'), may hold values from -3 to 3
Outputs:
- occupancy: bfloat16 [512, 65536], P('ch', 'az')
Inputs may be any that keep to these rules, and one draw needn't show every extreme that they name: `request_cell`: cell index a * 256 + r within the sector that the slot's block names; entries of slots that no corner_slot entry names are never read. `corner_slot`: within one tile the 2048 entries name distinct slots; at most 32 slots of one sector block are named, exactly 32 for some sector of every tile.
All inputs are finite; a program needn't handle non-finite values.
Results may differ from a plain program's by a relative error of at most 0.014.
Values may be sent and summed in bfloat16 or wider, within the bound.
A program may use at most 64 MiB of HBM per device.

v0:
```python
import jax
import jax.numpy as jnp
from jax import lax
from jax.sharding import PartitionSpec as P


def padded_2(array, sides, width):
    for axis, dim in sides:
        size, length = (lax.axis_size(axis), array.shape[dim])
        up = [(i, (i + 1) % size) for i in range(size)]
        down = [(j, i) for i, j in up]
        last = lax.slice_in_dim(array, length - width, length, axis=dim)
        first = lax.slice_in_dim(array, 0, width, axis=dim)
        before = lax.ppermute(last, axis, up)
        after = lax.ppermute(first, axis, down)
        array = jnp.concatenate([before, array, after], axis=dim)
    return array


def convolve(padded, weight, columns, ranges):
    inputs = padded.shape[0]
    ranged = jnp.pad(padded, ((0, 0), (0, 0), (1, 1)))
    running = jnp.zeros((weight.shape[0], columns * ranges), jnp.float32)
    for tap_az in range(3):
        for tap_rg in range(3):
            window = ranged[:, tap_az : tap_az + columns, tap_rg : tap_rg + ranges].reshape(
                inputs, columns * ranges
            )
            running = running + jnp.dot(
                weight[:, tap_az, tap_rg, :], window, preferred_element_type=jnp.float32
            )
    return running


def local(
    features,
    conv1_weight,
    conv1_bias,
    conv2_weight,
    conv2_bias,
    request_cell,
    corner_slot,
    corner_frac,
    expand_weight,
    expand_bias,
):
    columns = features.shape[1]
    ranges = features.shape[2]
    outputs = conv1_weight.shape[0]
    widened = padded_2(features, (("az", 1),), 1)
    hidden_one = jax.nn.relu(
        convolve(widened, conv1_weight, columns, ranges) + conv1_bias[:, None]
    ).astype(jnp.bfloat16)
    hidden_one = padded_2(hidden_one.reshape(outputs, columns, ranges), (("az", 1),), 1)
    second_sum = convolve(
        lax.all_gather(hidden_one, "ch", axis=0, tiled=True), conv2_weight, columns, ranges
    )
    hidden_two = jax.nn.relu(second_sum + conv2_bias[:, None]).astype(jnp.bfloat16)
    asked_cells = lax.all_to_all(request_cell, "az", split_axis=0, concat_axis=0, tiled=True)
    picked_cells = jnp.take(hidden_two, asked_cells, axis=1)
    arrived = lax.all_to_all(picked_cells, "az", split_axis=1, concat_axis=1, tiled=True)
    frac_range = corner_frac[0][None, :]
    frac_azim = corner_frac[1][None, :]
    weights = [
        (1.0 - frac_range) * (1.0 - frac_azim),
        frac_range * (1.0 - frac_azim),
        (1.0 - frac_range) * frac_azim,
        frac_range * frac_azim,
    ]
    resampled = jnp.zeros((outputs, corner_slot.shape[1]), jnp.float32)
    for k in range(4):
        resampled = resampled + weights[k] * jnp.take(arrived, corner_slot[k], axis=1).astype(
            jnp.float32
        )
    resampled = resampled.astype(jnp.bfloat16)
    share_rows = expand_weight.shape[1] // lax.axis_size("ch")
    partial_term = lax.dot_general(
        expand_weight, resampled, (((0,), (0,)), ((), ())), preferred_element_type=jnp.float32
    )
    summed = lax.psum(partial_term.astype(jnp.bfloat16), "ch").astype(jnp.float32)
    own_rows = lax.dynamic_slice_in_dim(summed, lax.axis_index("ch") * share_rows, share_rows, 0)
    return (own_rows + expand_bias[:, None]).astype(jnp.bfloat16)


def solution(mesh):
    return jax.shard_map(
        local,
        mesh=mesh,
        in_specs=(
            P(None, "az", None),
            P("ch", None, None, None),
            P("ch"),
            P("ch", None, None, None),
            P("ch"),
            P("az"),
            P(None, "az"),
            P(None, "az"),
            P("ch", None),
            P("ch"),
        ),
        out_specs=P("ch", "az"),
        check_vma=False,
    )
```

profile of v0, /device:TPU:1, one launch (start us, length us, event | category | flops | bytes accessed | tf_op | source)
XLA Modules:
  0.0 193.8 jit_solution(11583841178571506555)
XLA Ops:
  6.5 1.7 fusion.78
  8.3 5.0 %collective-permute-start = (bf16[256,1,256]{2,1,0:T(2,128)(2,1)S(1)}, bf16[256,1,256]{2,1,0:T(2,128)(2,1)S(1)}, u32[]{:S(2)}, u32[]{:S(2)}) collective-permute-start(bf16[256,1,256]{2,1,0:T(2,128)(2,1)S(1)} %get-tuple-element.23), channel_id=1, source_target_pairs={{0,4},{4,8},{8,12},{12,16},{16,20},{20,24},{24,28},{28,32},{32,36}... | collective-permute-start | bytes 393224 | tf_op jit(solution)/shard_map/ppermute | solution.py:14
  13.3 14.3 %collective-permute-start.1 = (bf16[256,1,256]{2,1,0:T(2,128)(2,1)S(1)}, bf16[256,1,256]{2,1,0:T(2,128)(2,1)S(1)}, u32[]{:S(2)}, u32[]{:S(2)}) collective-permute-start(bf16[256,1,256]{2,1,0:T(2,128)(2,1)S(1)} %get-tuple-element.24), channel_id=1, source_target_pairs={{4,0},{8,4},{12,8},{16,12},{20,16},{24,20},{28,24},{32,28},{36,32}... | collective-permute-start | bytes 393224 | tf_op jit(solution)/shard_map/ppermute | solution.py:15
  27.6 1.4 all_to_all.16
  29.0 8.9 %all-to-all-start = ((s32[128,32,1]{1,2,0:T(1,128)}), s32[128,32,1]{1,2,0:T(1,128)S(1)}, u32[]{:S(2)}, u32[]{:S(2)}) async-start(s32[128,32,1]{1,2,0:T(1,128)} %bitcast.2), calls=%async_computation | async-start | bytes 131072 | tf_op jit(solution)/shard_map/all_to_all | solution.py:59
  38.4 12.6 %all-to-all-done = s32[128,32,1]{1,2,0:T(1,128)S(1)} async-done(((s32[128,32,1]{1,2,0:T(1,128)}), s32[128,32,1]{1,2,0:T(1,128)S(1)}, u32[]{:S(2)}, u32[]{:S(2)}) %all-to-all-start) | async-done | bytes 16416 | tf_op jit(solution)/shard_map/all_to_all | solution.py:59
  51.0 0.5 broadcast.128
  51.5 0.8 reduce.3
  52.5 2.4 %fusion.5 = bf16[256,6,258]{2,1,0:T(8,128)(2,1)S(1)} fusion(bf16[256,1,256]{2,1,0:T(2,128)(2,1)S(1)} %collective-permute-done.1, bf16[256,4,256]{2,1,0:T(4,128)(2,1)S(1)} %copy-done.1, bf16[256,1,256]{2,1,0:T(2,128)(2,1)S(1)} %collective-permute-done), kind=kLoop, calls=%fused_computation.12 | loop fusion | flops 4755456 | bytes 1579008 | tf_op jit(solution)/shard_map/concatenate | solution.py:16
  54.9 1.8 fusion.77
  57.1 1.2 pad_maximum_fusion
  60.5 2.2 %collective-permute-start.2 = (bf16[64,1,256]{2,0,1:T(8,128)(2,1)S(1)}, bf16[64,1,256]{2,0,1:T(8,128)(2,1)S(1)}, u32[]{:S(2)}, u32[]{:S(2)}) collective-permute-start(bf16[64,1,256]{2,0,1:T(8,128)(2,1)S(1)} %get-tuple-element.25), channel_id=1, source_target_pairs={{0,4},{4,8},{8,12},{12,16},{16,20},{20,24},{24,28},{28,32},{32,36}... | collective-permute-start | bytes 98312 | tf_op jit(solution)/shard_map/ppermute | solution.py:14
  62.7 9.4 %collective-permute-start.3 = (bf16[64,1,256]{2,0,1:T(8,128)(2,1)S(1)}, bf16[64,1,256]{2,0,1:T(8,128)(2,1)S(1)}, u32[]{:S(2)}, u32[]{:S(2)}) collective-permute-start(bf16[64,1,256]{2,0,1:T(8,128)(2,1)S(1)} %get-tuple-element.26), channel_id=1, source_target_pairs={{4,0},{8,4},{12,8},{16,12},{20,16},{24,20},{28,24},{32,28},{36,32}... | collective-permute-start | bytes 98312 | tf_op jit(solution)/shard_map/ppermute | solution.py:15
  72.2 1.0 collective-permute-done.3
  73.2 11.6 %all_gather.3 = bf16[256,6,256]{2,0,1:T(8,128)(2,1)S(1)} all-gather(bf16[64,6,256]{2,0,1:T(8,128)(2,1)S(1)} %pad_maximum_fusion.2), channel_id=1, replica_groups=mesh['az'=128,'ch'=4] {'ch'}, dimensions={0}, use_global_device_ids=true | all-gather | bytes 983040 | tf_op jit(solution)/shard_map/all_gather | solution.py:56
  85.1 0.6 pad_slice_fusion
  85.7 0.3 copy-done.2
  86.3 0.3 convolution_add_fusion.10
  88.8 12.1 %gather_fusion = bf16[4096,64]{1,0:T(8,128)(2,1)S(1)} fusion(bf16[64,1024]{0,1:T(8,128)(2,1)S(1)} %copy.29, s32[4096]{0:T(1024)S(1)} %broadcast_clamp_fusion), kind=kCustom, calls=%fused_computation.4 | custom fusion | bytes 1064960 | tf_op jit(solution)/shard_map/jit(_take)/gather | solution.py:60
  100.9 0.8 fusion.81
  101.8 1.4 reshape.189
  103.1 12.0 %all-to-all-start.1 = ((bf16[128,2,1024]{2,1,0:T(2,128)(2,1)}), bf16[128,2,1024]{2,1,0:T(2,128)(2,1)S(1)}, u32[]{:S(2)}, u32[]{:S(2)}) async-start(bf16[128,2,1024]{2,1,0:T(2,128)(2,1)} %reshape.189), calls=%async_computation.1 | async-start | bytes 1048576 | tf_op jit(solution)/shard_map/all_to_all | solution.py:61
  115.3 19.0 %all-to-all-done.1 = bf16[128,2,1024]{2,1,0:T(2,128)(2,1)S(1)} async-done(((bf16[128,2,1024]{2,1,0:T(2,128)(2,1)}), bf16[128,2,1024]{2,1,0:T(2,128)(2,1)S(1)}, u32[]{:S(2)}, u32[]{:S(2)}) %all-to-all-start.1) | async-done | bytes 524320 | tf_op jit(solution)/shard_map/all_to_all | solution.py:61
  134.3 0.6 reshape.190
  134.9 1.3 gather_fusion.1
  136.2 1.3 gather_fusion.2
  137.6 1.3 gather_fusion.3
  138.9 1.3 gather_fusion.4
  140.3 1.7 fusion.6
  142.0 43.2 %all-reduce.4.cloned.1.call-done = bf16[512,512]{0,1:T(8,128)(2,1)} async-done(((bf16[512,512]{0,1:T(8,128)(2,1)}), bf16[512,512]{0,1:T(8,128)(2,1)}) %all-reduce.4.cloned.1.call-update) | async-done | bytes 524304 | tf_op jit(solution)/shard_map/psum | solution.py:80
  185.3 0.9 add_convert_fusion
  186.2 0.8 copy.30
  (69 shorter events, 5.8 us)
Async XLA Ops:
  6.5 133.8 %copy-start = (bf16[64,512]{1,0:T(8,128)(2,1)S(1)}, bf16[64,512]{1,0:T(8,128)(2,1)}, u32[]{:S(2)}) copy-start(bf16[64,512]{1,0:T(8,128)(2,1)} %param.20) | copy-start | bytes 196612
  6.5 31.4 %copy-start.1 = (bf16[256,4,256]{2,1,0:T(4,128)(2,1)S(1)}, bf16[256,4,256]{2,1,0:T(4,128)(2,1)}, u32[]{:S(2)}) copy-start(bf16[256,4,256]{2,1,0:T(4,128)(2,1)} %param.12) | copy-start | bytes 1572868
  6.5 31.5 %copy-start.4 = (s32[4,512]{1,0:T(4,128)S(1)}, s32[4,512]{1,0:T(4,128)}, u32[]{:S(2)}) copy-start(s32[4,512]{1,0:T(4,128)} %param.18) | copy-start | bytes 24580
  6.5 31.6 %copy-start.3 = (bf16[64,3,3,256]{3,0,2,1:T(8,128)(2,1)S(1)}, bf16[64,3,3,256]{3,0,2,1:T(8,128)(2,1)}, u32[]{:S(2)}) copy-start(bf16[64,3,3,256]{3,0,2,1:T(8,128)(2,1)} %param.13) | copy-start | bytes 884740
  8.3 44.2 %collective-permute-start = (bf16[256,1,256]{2,1,0:T(2,128)(2,1)S(1)}, bf16[256,1,256]{2,1,0:T(2,128)(2,1)S(1)}, u32[]{:S(2)}, u32[]{:S(2)}) collective-permute-start(bf16[256,1,256]{2,1,0:T(2,128)(2,1)S(1)} %get-tuple-element.23), channel_id=1, source_target_pairs={{0,4},{4,8},{8,12},{12,16},{16,20},{20,24},{24,28},{28,32},{32,36}... | collective-permute-start | bytes 393224 | tf_op jit(solution)/shard_map/ppermute | solution.py:14
  13.3 39.2 %collective-permute-start.1 = (bf16[256,1,256]{2,1,0:T(2,128)(2,1)S(1)}, bf16[256,1,256]{2,1,0:T(2,128)(2,1)S(1)}, u32[]{:S(2)}, u32[]{:S(2)}) collective-permute-start(bf16[256,1,256]{2,1,0:T(2,128)(2,1)S(1)} %get-tuple-element.24), channel_id=1, source_target_pairs={{4,0},{8,4},{12,8},{16,12},{20,16},{24,20},{28,24},{32,28},{36,32}... | collective-permute-start | bytes 393224 | tf_op jit(solution)/shard_map/ppermute | solution.py:15
  29.0 22.0 %all-to-all-start = ((s32[128,32,1]{1,2,0:T(1,128)}), s32[128,32,1]{1,2,0:T(1,128)S(1)}, u32[]{:S(2)}, u32[]{:S(2)}) async-start(s32[128,32,1]{1,2,0:T(1,128)} %bitcast.2), calls=%async_computation | async-start | bytes 131072 | tf_op jit(solution)/shard_map/all_to_all | solution.py:59
  59.6 0.7 copy-start.6
  60.5 11.6 %collective-permute-start.2 = (bf16[64,1,256]{2,0,1:T(8,128)(2,1)S(1)}, bf16[64,1,256]{2,0,1:T(8,128)(2,1)S(1)}, u32[]{:S(2)}, u32[]{:S(2)}) collective-permute-start(bf16[64,1,256]{2,0,1:T(8,128)(2,1)S(1)} %get-tuple-element.25), channel_id=1, source_target_pairs={{0,4},{4,8},{8,12},{12,16},{16,20},{20,24},{24,28},{28,32},{32,36}... | collective-permute-start | bytes 98312 | tf_op jit(solution)/shard_map/ppermute | solution.py:14
  62.7 10.4 %collective-permute-start.3 = (bf16[64,1,256]{2,0,1:T(8,128)(2,1)S(1)}, bf16[64,1,256]{2,0,1:T(8,128)(2,1)S(1)}, u32[]{:S(2)}, u32[]{:S(2)}) collective-permute-start(bf16[64,1,256]{2,0,1:T(8,128)(2,1)S(1)} %get-tuple-element.26), channel_id=1, source_target_pairs={{4,0},{8,4},{12,8},{16,12},{20,16},{24,20},{28,24},{32,28},{36,32}... | collective-permute-start | bytes 98312 | tf_op jit(solution)/shard_map/ppermute | solution.py:15
  85.0 1.0 copy-start.2
  87.4 0.9 copy-start.7
  101.7 13.5 %copy-start.5 = (f32[2,512]{1,0:T(2,128)S(1)}, f32[2,512]{1,0:T(2,128)}, u32[]{:S(2)}) copy-start(f32[2,512]{1,0:T(2,128)} %param.19) | copy-start | bytes 12292
  103.1 31.1 %all-to-all-start.1 = ((bf16[128,2,1024]{2,1,0:T(2,128)(2,1)}), bf16[128,2,1024]{2,1,0:T(2,128)(2,1)S(1)}, u32[]{:S(2)}, u32[]{:S(2)}) async-start(bf16[128,2,1024]{2,1,0:T(2,128)(2,1)} %reshape.189), calls=%async_computation.1 | async-start | bytes 1048576 | tf_op jit(solution)/shard_map/all_to_all | solution.py:61
  115.1 70.1 %all-reduce.4.cloned.1.call-start = ((), (), s32[]{:S(2)}) async-start(), calls=%async_computation.2 | async-start | bytes 1048576 | tf_op jit(solution)/shard_map/psum | solution.py:80
  137.6 47.7 %copy-start.8 = (f32[128]{0:T(128)S(1)}, f32[128]{0:T(128)}, u32[]{:S(2)}) copy-start(f32[128]{0:T(128)} %param.21) | copy-start | bytes 1540
Sparse Core Ops, SparseCore 0:
  142.1 43.0 all-reduce.3
where the time goes:
time: 194 us
  waiting for transfers between devices  75.9 us (39%)
  starting transfers between devices  51.8 us (27%)
  local copies, waits for them, and re-layouts  28.1 us (14%)
  between operations  14 us (7%)
  blocking collectives  11.6 us (6%)
  other arithmetic  6.25 us (3%)
  matrix products  6.14 us (3%)
    psum x1, waiting for transfers between devices, local(): lax.psum(partial_term.astype(jnp.bfloat16), 'ch').astype(jnp.float32)  43.2 us
    ppermute x2, starting transfers between devices, padded_2(): after = lax.ppermute(first, axis, down)  23.7 us
    all_to_all x1, waiting for transfers between devices, local(): lax.all_to_all(picked_cells, 'az', split_axis=1, concat_axis=1, tiled=True)  19 us
    all_to_all x1, waiting for transfers between devices, local(): lax.all_to_all(request_cell, 'az', split_axis=0, concat_axis=0, tiled=True)  12.6 us
    gather x1, local copies, waits for them, and re-layouts, local(): picked_cells = jnp.take(hidden_two, asked_cells, axis=1)  12.1 us
    all_to_all x1, starting transfers between devices, local(): lax.all_to_all(picked_cells, 'az', split_axis=1, concat_axis=1, tiled=True)  12 us
    all_gather x1, blocking collectives, local(): lax.all_gather(hidden_one, 'ch', axis=0, tiled=True)  11.6 us
    all_to_all x1, starting transfers between devices, local(): lax.all_to_all(request_cell, 'az', split_axis=0, concat_axis=0, tiled=True)  8.91 us
  transfers between devices with their start and end apart: 7, of which 4 were waited for; matrix products, arithmetic and copies ran while one was open for 1% of the time, Pallas kernels for 0%

commit v1 on v0

--- a/solution.py
+++ b/solution.py
@@ -44,6 +44,12 @@
     expand_weight,
     expand_bias,
 ):
+
+    def begin_slot(original, mesh_dim):
+        wide_out = lax.all_gather(original, mesh_dim)
+        reply = jnp.sum(wide_out, axis=0)
+        return reply
+
     columns = features.shape[1]
     ranges = features.shape[2]
     outputs = conv1_weight.shape[0]
@@ -77,7 +83,7 @@
     partial_term = lax.dot_general(
         expand_weight, resampled, (((0,), (0,)), ((), ())), preferred_element_type=jnp.float32
     )
-    summed = lax.psum(partial_term.astype(jnp.bfloat16), "ch").astype(jnp.float32)
+    summed = begin_slot(partial_term.astype(jnp.bfloat16), "ch").astype(jnp.float32)
     own_rows = lax.dynamic_slice_in_dim(summed, lax.axis_index("ch") * share_rows, share_rows, 0)
     return (own_rows + expand_bias[:, None]).astype(jnp.bfloat16)
 

time: 194 us -> 186 us (0.959)
  waiting for transfers between devices: 75.9 us -> 61.2 us
  local copies, waits for them, and re-layouts: 28.1 us -> 32.5 us
    psum x1 -> x0, waiting for transfers between devices: 43.2 us -> none  [local(): lax.psum(partial_term.astype(jnp.bfloat16), 'ch').astype(jnp.float32)]
    all_gather x0 -> x1, waiting for transfers between devices: none -> 29.6 us  [begin_slot(): wide_out = lax.all_gather(original, mesh_dim)]
    all_gather x0 -> x1, local copies, waits for them, and re-layouts: none -> 3.31 us  [begin_slot(): wide_out = lax.all_gather(original, mesh_dim)]
    reduce_sum x0 -> x1, other arithmetic: none -> 2.8 us  [begin_slot(): reply = jnp.sum(wide_out, axis=0)]
  transfers between devices with their start and end apart: 7 -> 7, of which waited for: 4 -> 4; matrix products, arithmetic and copies ran while one was open for 1% -> 2% of each run, Pallas kernels for 0% -> 0%
where the time goes in v1:
time: 186 us; the launch traced here: 185 us
  waiting for transfers between devices  61.2 us (33%)
  starting transfers between devices  51.8 us (28%)
  local copies, waits for them, and re-layouts  32.5 us (17%)
  between operations  14 us (8%)
  blocking collectives  11.6 us (6%)
  other arithmetic  8.15 us (4%)
  matrix products  6.15 us (3%)
    all_gather x1, waiting for transfers between devices, begin_slot(): wide_out = lax.all_gather(original, mesh_dim)  29.6 us
    ppermute x2, starting transfers between devices, padded_2(): after = lax.ppermute(first, axis, down)  23.7 us
    all_to_all x1, waiting for transfers between devices, local(): lax.all_to_all(picked_cells, 'az', split_axis=1, concat_axis=1, tiled=True)  19 us
    gather x1, local copies, waits for them, and re-layouts, local(): picked_cells = jnp.take(hidden_two, asked_cells, axis=1)  12.1 us
    all_to_all x1, starting transfers between devices, local(): lax.all_to_all(picked_cells, 'az', split_axis=1, concat_axis=1, tiled=True)  12 us
    all_to_all x1, waiting for transfers between devices, local(): lax.all_to_all(request_cell, 'az', split_axis=0, concat_axis=0, tiled=True)  11.6 us
    all_gather x1, blocking collectives, local(): lax.all_gather(hidden_one, 'ch', axis=0, tiled=True)  11.6 us
    all_to_all x1, starting transfers between devices, local(): lax.all_to_all(request_cell, 'az', split_axis=0, concat_axis=0, tiled=True)  8.91 us
  transfers between devices with their start and end apart: 7, of which 4 were waited for; matrix products, arithmetic and copies ran while one was open for 2% of the time, Pallas kernels for 0%

profile of v1, /device:TPU:1, one launch (start us, length us, event | category | flops | bytes accessed | tf_op | source)
XLA Modules:
  0.0 185.5 jit_solution(11710892635472603982)
XLA Ops:
  6.5 1.8 fusion.78
  8.3 5.0 %collective-permute-start = (bf16[256,1,256]{2,1,0:T(2,128)(2,1)S(1)}, bf16[256,1,256]{2,1,0:T(2,128)(2,1)S(1)}, u32[]{:S(2)}, u32[]{:S(2)}) collective-permute-start(bf16[256,1,256]{2,1,0:T(2,128)(2,1)S(1)} %get-tuple-element.23), channel_id=1, source_target_pairs={{0,4},{4,8},{8,12},{12,16},{16,20},{20,24},{24,28},{28,32},{32,36}... | collective-permute-start | bytes 393224 | tf_op jit(solution)/shard_map/ppermute | solution.py:14
  13.4 14.3 %collective-permute-start.1 = (bf16[256,1,256]{2,1,0:T(2,128)(2,1)S(1)}, bf16[256,1,256]{2,1,0:T(2,128)(2,1)S(1)}, u32[]{:S(2)}, u32[]{:S(2)}) collective-permute-start(bf16[256,1,256]{2,1,0:T(2,128)(2,1)S(1)} %get-tuple-element.24), channel_id=1, source_target_pairs={{4,0},{8,4},{12,8},{16,12},{20,16},{24,20},{28,24},{32,28},{36,32}... | collective-permute-start | bytes 393224 | tf_op jit(solution)/shard_map/ppermute | solution.py:15
  27.6 1.4 all_to_all.16
  29.1 8.9 %all-to-all-start = ((s32[128,32,1]{1,2,0:T(1,128)}), s32[128,32,1]{1,2,0:T(1,128)S(1)}, u32[]{:S(2)}, u32[]{:S(2)}) async-start(s32[128,32,1]{1,2,0:T(1,128)} %bitcast.2), calls=%async_computation | async-start | bytes 131072 | tf_op jit(solution)/shard_map/all_to_all | solution.py:65
  38.0 1.1 copy.34
  39.4 11.6 %all-to-all-done = s32[128,32,1]{1,2,0:T(1,128)S(1)} async-done(((s32[128,32,1]{1,2,0:T(1,128)}), s32[128,32,1]{1,2,0:T(1,128)S(1)}, u32[]{:S(2)}, u32[]{:S(2)}) %all-to-all-start) | async-done | bytes 16416 | tf_op jit(solution)/shard_map/all_to_all | solution.py:65
  51.0 0.5 broadcast.128
  51.5 0.8 reduce.4
  52.5 2.4 %fusion.5 = bf16[256,6,258]{2,1,0:T(8,128)(2,1)S(1)} fusion(bf16[256,1,256]{2,1,0:T(2,128)(2,1)S(1)} %collective-permute-done.1, bf16[256,4,256]{2,1,0:T(4,128)(2,1)S(1)} %copy-done.1, bf16[256,1,256]{2,1,0:T(2,128)(2,1)S(1)} %collective-permute-done), kind=kLoop, calls=%fused_computation.12 | loop fusion | flops 4755456 | bytes 1579008 | tf_op jit(solution)/shard_map/concatenate | solution.py:16
  54.9 1.8 fusion.77
  57.1 1.2 pad_maximum_fusion
  60.5 2.2 %collective-permute-start.2 = (bf16[64,1,256]{2,0,1:T(8,128)(2,1)S(1)}, bf16[64,1,256]{2,0,1:T(8,128)(2,1)S(1)}, u32[]{:S(2)}, u32[]{:S(2)}) collective-permute-start(bf16[64,1,256]{2,0,1:T(8,128)(2,1)S(1)} %get-tuple-element.25), channel_id=1, source_target_pairs={{0,4},{4,8},{8,12},{12,16},{16,20},{20,24},{24,28},{28,32},{32,36}... | collective-permute-start | bytes 98312 | tf_op jit(solution)/shard_map/ppermute | solution.py:14
  62.8 9.4 %collective-permute-start.3 = (bf16[64,1,256]{2,0,1:T(8,128)(2,1)S(1)}, bf16[64,1,256]{2,0,1:T(8,128)(2,1)S(1)}, u32[]{:S(2)}, u32[]{:S(2)}) collective-permute-start(bf16[64,1,256]{2,0,1:T(8,128)(2,1)S(1)} %get-tuple-element.26), channel_id=1, source_target_pairs={{4,0},{8,4},{12,8},{16,12},{20,16},{24,20},{28,24},{32,28},{36,32}... | collective-permute-start | bytes 98312 | tf_op jit(solution)/shard_map/ppermute | solution.py:15
  72.2 1.0 collective-permute-done.3
  73.2 11.6 %all_gather.9 = bf16[256,6,256]{2,0,1:T(8,128)(2,1)S(1)} all-gather(bf16[64,6,256]{2,0,1:T(8,128)(2,1)S(1)} %pad_maximum_fusion.2), channel_id=1, replica_groups=mesh['az'=128,'ch'=4] {'ch'}, dimensions={0}, use_global_device_ids=true | all-gather | bytes 983040 | tf_op jit(solution)/shard_map/all_gather | solution.py:62
  85.1 0.6 pad_slice_fusion
  88.8 12.1 %gather_fusion = bf16[4096,64]{1,0:T(8,128)(2,1)S(1)} fusion(bf16[64,1024]{0,1:T(8,128)(2,1)S(1)} %copy.27, s32[4096]{0:T(1024)S(1)} %broadcast_clamp_fusion), kind=kCustom, calls=%fused_computation.4 | custom fusion | bytes 1064960 | tf_op jit(solution)/shard_map/jit(_take)/gather | solution.py:66
  101.0 0.8 fusion.81
  101.8 1.4 reshape.190
  103.2 12.0 %all-to-all-start.1 = ((bf16[128,2,1024]{2,1,0:T(2,128)(2,1)}), bf16[128,2,1024]{2,1,0:T(2,128)(2,1)S(1)}, u32[]{:S(2)}, u32[]{:S(2)}) async-start(bf16[128,2,1024]{2,1,0:T(2,128)(2,1)} %reshape.190), calls=%async_computation.1 | async-start | bytes 1048576 | tf_op jit(solution)/shard_map/all_to_all | solution.py:67
  115.3 19.0 %all-to-all-done.1 = bf16[128,2,1024]{2,1,0:T(2,128)(2,1)S(1)} async-done(((bf16[128,2,1024]{2,1,0:T(2,128)(2,1)}), bf16[128,2,1024]{2,1,0:T(2,128)(2,1)S(1)}, u32[]{:S(2)}, u32[]{:S(2)}) %all-to-all-start.1) | async-done | bytes 524320 | tf_op jit(solution)/shard_map/all_to_all | solution.py:67
  134.3 0.6 reshape.191
  134.9 1.3 gather_fusion.1
  136.3 1.3 gather_fusion.2
  137.6 1.3 gather_fusion.3
  139.0 1.3 gather_fusion.4
  140.3 1.7 fusion.6
  142.1 29.6 %all-gather.3.cloned.1.call-done = bf16[2048,512]{0,1:T(8,128)(2,1)} async-done(((bf16[512,512]{0,1:T(8,128)(2,1)}), bf16[2048,512]{0,1:T(8,128)(2,1)}) %all-gather.3.cloned.1.call-update) | async-done | bytes 2097168 | tf_op jit(solution)/shard_map/all_gather | solution.py:49
  171.7 3.3 %reshape.168 = bf16[4,512,512]{1,0,2:T(4,128)(2,1)S(1)} reshape(bf16[2048,512]{0,1:T(8,128)(2,1)} %all-gather.3.cloned.1.call-done) | data formatting | bytes 4194304 | tf_op jit(solution)/shard_map/all_gather | solution.py:49
  175.0 2.8 %reduce_sum.12 = bf16[512,512]{0,1:T(8,128)(2,1)S(1)} reduce(bf16[4,512,512]{1,0,2:T(4,128)(2,1)S(1)} %reshape.168, bf16[]{:T(256)} %constant.26.clone.1), dimensions={0}, to_apply=%region_0.2 | reduce | flops 786432 | bytes 2621442 | tf_op jit(solution)/shard_map/reduce_sum | solution.py:50
  177.9 0.8 copy.28
  (71 shorter events, 6.4 us)
Async XLA Ops:
  6.5 133.8 %copy-start = (bf16[64,512]{1,0:T(8,128)(2,1)S(1)}, bf16[64,512]{1,0:T(8,128)(2,1)}, u32[]{:S(2)}) copy-start(bf16[64,512]{1,0:T(8,128)(2,1)} %param.20) | copy-start | bytes 196612
  6.5 46.0 %copy-start.1 = (bf16[256,4,256]{2,1,0:T(4,128)(2,1)S(1)}, bf16[256,4,256]{2,1,0:T(4,128)(2,1)}, u32[]{:S(2)}) copy-start(bf16[256,4,256]{2,1,0:T(4,128)(2,1)} %param.12) | copy-start | bytes 1572868
  6.5 32.6 %copy-start.4 = (s32[4,512]{1,0:T(4,128)S(1)}, s32[4,512]{1,0:T(4,128)}, u32[]{:S(2)}) copy-start(s32[4,512]{1,0:T(4,128)} %param.18) | copy-start | bytes 24580
  6.5 32.6 %copy-start.3 = (bf16[64,3,3,256]{3,0,2,1:T(8,128)(2,1)S(1)}, bf16[64,3,3,256]{3,0,2,1:T(8,128)(2,1)}, u32[]{:S(2)}) copy-start(bf16[64,3,3,256]{3,0,2,1:T(8,128)(2,1)} %param.13) | copy-start | bytes 884740
  8.3 44.2 %collective-permute-start = (bf16[256,1,256]{2,1,0:T(2,128)(2,1)S(1)}, bf16[256,1,256]{2,1,0:T(2,128)(2,1)S(1)}, u32[]{:S(2)}, u32[]{:S(2)}) collective-permute-start(bf16[256,1,256]{2,1,0:T(2,128)(2,1)S(1)} %get-tuple-element.23), channel_id=1, source_target_pairs={{0,4},{4,8},{8,12},{12,16},{16,20},{20,24},{24,28},{28,32},{32,36}... | collective-permute-start | bytes 393224 | tf_op jit(solution)/shard_map/ppermute | solution.py:14
  13.4 39.2 %collective-permute-start.1 = (bf16[256,1,256]{2,1,0:T(2,128)(2,1)S(1)}, bf16[256,1,256]{2,1,0:T(2,128)(2,1)S(1)}, u32[]{:S(2)}, u32[]{:S(2)}) collective-permute-start(bf16[256,1,256]{2,1,0:T(2,128)(2,1)S(1)} %get-tuple-element.24), channel_id=1, source_target_pairs={{4,0},{8,4},{12,8},{16,12},{20,16},{24,20},{28,24},{32,28},{36,32}... | collective-permute-start | bytes 393224 | tf_op jit(solution)/shard_map/ppermute | solution.py:15
  29.1 22.0 %all-to-all-start = ((s32[128,32,1]{1,2,0:T(1,128)}), s32[128,32,1]{1,2,0:T(1,128)S(1)}, u32[]{:S(2)}, u32[]{:S(2)}) async-start(s32[128,32,1]{1,2,0:T(1,128)} %bitcast.2), calls=%async_computation | async-start | bytes 131072 | tf_op jit(solution)/shard_map/all_to_all | solution.py:65
  59.4 0.9 copy-start.6
  60.5 11.6 %collective-permute-start.2 = (bf16[64,1,256]{2,0,1:T(8,128)(2,1)S(1)}, bf16[64,1,256]{2,0,1:T(8,128)(2,1)S(1)}, u32[]{:S(2)}, u32[]{:S(2)}) collective-permute-start(bf16[64,1,256]{2,0,1:T(8,128)(2,1)S(1)} %get-tuple-element.25), channel_id=1, source_target_pairs={{0,4},{4,8},{8,12},{12,16},{16,20},{20,24},{24,28},{28,32},{32,36}... | collective-permute-start | bytes 98312 | tf_op jit(solution)/shard_map/ppermute | solution.py:14
  62.8 10.4 %collective-permute-start.3 = (bf16[64,1,256]{2,0,1:T(8,128)(2,1)S(1)}, bf16[64,1,256]{2,0,1:T(8,128)(2,1)S(1)}, u32[]{:S(2)}, u32[]{:S(2)}) collective-permute-start(bf16[64,1,256]{2,0,1:T(8,128)(2,1)S(1)} %get-tuple-element.26), channel_id=1, source_target_pairs={{4,0},{8,4},{12,8},{16,12},{20,16},{24,20},{28,24},{32,28},{36,32}... | collective-permute-start | bytes 98312 | tf_op jit(solution)/shard_map/ppermute | solution.py:15
  85.1 1.0 copy-start.2
  87.2 1.2 copy-start.7
  101.0 14.3 %copy-start.5 = (f32[2,512]{1,0:T(2,128)S(1)}, f32[2,512]{1,0:T(2,128)}, u32[]{:S(2)}) copy-start(f32[2,512]{1,0:T(2,128)} %param.19) | copy-start | bytes 12292
  103.2 31.1 %all-to-all-start.1 = ((bf16[128,2,1024]{2,1,0:T(2,128)(2,1)}), bf16[128,2,1024]{2,1,0:T(2,128)(2,1)S(1)}, u32[]{:S(2)}, u32[]{:S(2)}) async-start(bf16[128,2,1024]{2,1,0:T(2,128)(2,1)} %reshape.190), calls=%async_computation.1 | async-start | bytes 1048576 | tf_op jit(solution)/shard_map/all_to_all | solution.py:67
  115.2 56.5 %all-gather.3.cloned.1.call-start = ((), (), s32[]{:S(2)}) async-start(), calls=%async_computation.2 | async-start | bytes 2621440 | tf_op jit(solution)/shard_map/all_gather | solution.py:49
  175.0 2.8 %copy-start.8 = (f32[128]{0:T(128)S(1)}, f32[128]{0:T(128)}, u32[]{:S(2)}) copy-start(f32[128]{0:T(128)} %param.21) | copy-start | bytes 1540
Sparse Core Ops, SparseCore 0:
  142.2 29.4 all-gather.2
